TPU v7x, 512 devices: a whole 4x4x16 slice. The times are simulated.
512 devices in a mesh: ex: 32 (over y, x, core), tp: 16 (over z).
Axes of the slice: x: 4, y: 4, z: 16, core: 2. Of those that a mesh axis runs over, the one named last changes fastest.
Arguments:
- activations: bfloat16 [16384, 8192], P('ex', 'tp'), may hold values from -6 to 6
- out_grads: bfloat16 [16384, 29568], P('ex', 'tp'), may hold values from -6 to 6
- basis_in: bfloat16 [8192, 512], P('tp', 'ex'), may hold values from -0.0625 to 0.0625
- basis_out: bfloat16 [29568, 512], P('tp', 'ex'), may hold values from -0.03125 to 0.03125
- eigen: float32 [512, 512], replicated, may hold values from 1 to 10
- lengths: int32 [32], P('ex'), may hold values from 64 to 512, as said below
- query_in: bfloat16 [512, 8192], P(None, 'tp'), may hold values from -0.09375 to 0.09375
- query_out: bfloat16 [512, 8192], P(None, 'tp'), may hold values from -0.09375 to 0.09375
Outputs:
- scores: float32 [32, 1024], P('ex', 'tp')
Inputs may be any that keep to these rules, and one draw needn't show every extreme that they name: `lengths`: some sequence has all 512 tokens counted in every draw.
All inputs are finite; a program needn't handle non-finite values.
Results may differ from a plain program's by a relative error of at most 0.0049.
Values may be sent and summed in bfloat16 or wider, within the bound.
No kernel may reach another device: no remote copies, remote signals or barrier semaphores. Data moves between devices by JAX's collectives and lax.ppermute only.
A program may use at most 64 MiB of HBM per device.

v0:
```python
import jax
import jax.numpy as jnp
from jax import lax
from jax.sharding import PartitionSpec as P

RANK = 8


DAMP = 0.1


def rotated_block(rounded, offset, seq_length, split_at):
    row_count = rounded.shape[0]
    positions = offset + lax.broadcasted_iota(jnp.int32, (row_count, 1), 0)
    kept_rows = (positions < seq_length).astype(jnp.bfloat16)
    inputs_side = rounded[:, :split_at]
    outputs_side = rounded[:, split_at:] * kept_rows
    return lax.dot_general(
        inputs_side, outputs_side, (((0,), (0,)), ((), ())), preferred_element_type=jnp.float32
    )


def shards(activations, out_grads, basis_in, basis_out, eigen, lengths, query_in, query_out):
    rotated_in = jnp.dot(
        activations,
        lax.all_gather(basis_in, "ex", axis=1, tiled=True),
        preferred_element_type=jnp.float32,
    )
    rotated_out = jnp.dot(
        out_grads,
        lax.all_gather(basis_out, "ex", axis=1, tiled=True),
        preferred_element_type=jnp.float32,
    )
    joined = jnp.concatenate([rotated_in, rotated_out], axis=1)
    split_at = rotated_in.shape[1]
    seq_length = lengths[0]
    shares = lax.psum_scatter(joined, "tp", scatter_dimension=0, tiled=True).astype(jnp.bfloat16)
    offset = lax.axis_index("tp") * shares.shape[0]
    statistic = lax.psum(rotated_block(shares, offset, seq_length, split_at), "tp")
    scaled = (statistic / (eigen + DAMP)).astype(jnp.bfloat16)
    weighted = jnp.dot(scaled, query_out, preferred_element_type=jnp.float32)
    summed = jnp.sum(weighted * query_in.astype(jnp.float32), axis=0)
    return summed.reshape(-1, RANK).sum(axis=1)[None, :]


def solution(mesh):
    in_specs = (
        P("ex", "tp"),
        P("ex", "tp"),
        P("tp", "ex"),
        P("tp", "ex"),
        P(),
        P("ex"),
        P(None, "tp"),
        P(None, "tp"),
    )
    out_specs = P("ex", "tp")
    return jax.shard_map(shards, mesh=mesh, in_specs=in_specs, out_specs=out_specs, check_vma=False)
```

profile of v0, /device:TPU:2, one launch (start us, length us, event | category | flops | bytes accessed | tf_op | source)
XLA Modules:
  0.0 302.7 jit_solution(5831505273846158410)
XLA Ops:
  6.5 0.0 copy-start
  6.5 0.0 all-gather.2.cloned.1.call-start
  6.5 0.7 all-gather.2.cloned.1.call-update
  7.3 0.0 reduce-scatter.4.cloned.1.call-start
  7.3 27.7 %all_gather.6 = bf16[512,512]{0,1:T(8,128)(2,1)S(1)} all-gather(bf16[512,16]{0,1:T(8,128)(2,1)} %param.10), channel_id=1, replica_groups=mesh['ex'=32,'tp'=16] {'ex'}, dimensions={1}, use_global_device_ids=true | all-gather | bytes 540672 | tf_op jit(solution)/shard_map/all_gather | solution.py:26
  35.0 1.5 fusion.6
  36.5 37.1 %all-gather.2.cloned.1.call-done = bf16[1848,512]{0,1:T(8,128)(2,1)} async-done(((bf16[1848,16]{0,1:T(8,128)(2,1)}), bf16[1848,512]{0,1:T(8,128)(2,1)}) %all-gather.2.cloned.1.call-update) | async-done | bytes 1892368 | tf_op jit(solution)/shard_map/all_gather | solution.py:31
  73.6 0.0 copy-done
  73.6 2.8 fusion.7
  76.4 1.5 pad_maximum_fusion
  77.9 2.9 copy.9
  80.8 0.0 copy-start.1
  80.8 0.0 reduce-scatter.4.cloned.1.call-update
  80.9 0.0 all-reduce.2.cloned.1.call-start
  81.6 72.4 %reduce-scatter.4.cloned.1.call-done = f32[32,1024]{1,0:T(8,128)} async-done(((f32[512,1024]{1,0:T(8,128)}), f32[32,1024]{1,0:T(8,128)}) %reduce-scatter.4.cloned.1.call-update) | async-done | bytes 131088
  154.1 1.1 copy.10
  155.2 1.3 fusion.2
  156.5 0.0 all-reduce.2.cloned.1.call-update
  156.5 136.9 %all-reduce.2.cloned.1.call-done = f32[512,512]{1,0:T(8,128)} async-done(((f32[512,512]{1,0:T(8,128)}), f32[512,512]{1,0:T(8,128)}) %all-reduce.2.cloned.1.call-update) | async-done | bytes 1048592 | tf_op jit(solution)/shard_map/psum | solution.py:39
  293.5 0.0 copy-done.1
  293.5 2.0 fusion
  295.5 0.1 reshape.12
  295.6 0.6 reduce_sum.19
  (1 shorter events, 0.0 us)
Async XLA Ops:
  6.5 67.1 %copy-start = (bf16[512,1848]{0,1:T(8,128)(2,1)S(1)}, bf16[512,1848]{0,1:T(8,128)(2,1)}, u32[]{:S(2)}) copy-start(bf16[512,1848]{0,1:T(8,128)(2,1)} %param.9) | copy-start | bytes 5677060
  6.5 67.1 %all-gather.2.cloned.1.call-start = ((), (), s32[]{:S(2)}) async-start(), calls=%async_computation.1 | async-start | bytes 2027520 | tf_op jit(solution)/shard_map/all_gather | solution.py:31
  7.3 146.8 %reduce-scatter.4.cloned.1.call-start = ((), (), s32[]{:S(2)}) async-start(), calls=%async_computation.3 | async-start | bytes 2228224
  80.8 212.6 %copy-start.1 = (f32[512,512]{1,0:T(8,128)S(1)}, f32[512,512]{1,0:T(8,128)}, u32[]{:S(2)}) copy-start(f32[512,512]{1,0:T(8,128)} %param.12) | copy-start | bytes 3145732
  80.9 212.6 %all-reduce.2.cloned.1.call-start = ((), (), s32[]{:S(2)}) async-start(), calls=%async_computation.2 | async-start | bytes 2097152 | tf_op jit(solution)/shard_map/psum | solution.py:39
Sparse Core Ops, SparseCore 0:
  10.6 63.0 all-gather.1
  81.0 73.0 reduce-scatter.3
  156.6 136.7 all-reduce.1
where the time goes:
time: 303 us
  waiting for transfers between devices  247 us (82%)
  blocking collectives  27.7 us (9%)
  between operations  13.9 us (5%)
  matrix products  7.63 us (3%)
  local copies, waits for them, and re-layouts  4.12 us (1%)
    psum x1, waiting for transfers between devices, shards(): lax.psum(rotated_block(shares, offset, seq_length, split_at), 'tp')  137 us
    unnamed x4, waiting for transfers between devices  73.2 us
    all_gather x1, waiting for transfers between devices, shards(): lax.all_gather(basis_out, 'ex', axis=1, tiled=True)  37.1 us
    all_gather x1, blocking collectives, shards(): lax.all_gather(basis_in, 'ex', axis=1, tiled=True)  27.7 us
  transfers between devices with their start and end apart: 3, of which 3 were waited for; matrix products, arithmetic and copies ran while one was open for 0% of the time, Pallas kernels for 0%

commit v1 on v0

v1 whole, which is shorter than its diff:
```python
import jax
import jax.numpy as jnp
from jax import lax
from jax.sharding import Mesh
from jax.sharding import PartitionSpec as P

RANK = 8
DAMP = 0.1
RING = 16
PLANE = ("y", "x")
LINE = ("c", "z")


def shift(x, forward, backward):
    pairs = []
    for core, step in enumerate((forward, backward)):
        for at in range(RING):
            pairs.append((core * RING + at, core * RING + (at + step) % RING))
    return lax.ppermute(x, LINE, pairs)


def whole_basis(columns):
    kept, width = columns.shape
    near = lax.all_to_all(jnp.broadcast_to(columns[None], (16, kept, width)), PLANE, 0, 0)
    far = lax.ppermute(near, "c", [(0, 1), (1, 0)])
    first = lax.axis_index("c") == 0
    both = jnp.stack([jnp.where(first, near, far), jnp.where(first, far, near)], axis=1)
    return both.reshape(-1, width)


def reduce_step(parts, near, far):
    own = parts[0]
    one = shift(parts[1], near, -near)
    two = shift(parts[2], -near, near)
    three = shift(parts[3], far, -far)
    f = jnp.float32
    return own + one.astype(f) + two.astype(f) + three.astype(f)


def shards(activations, out_grads, basis_in, basis_out, eigen, lengths, query_in, query_out):
    f32, bf16, f16 = jnp.float32, jnp.bfloat16, jnp.float16
    at = lax.axis_index("z")
    low, high = at % 4, at // 4
    depth = basis_in.shape[0]
    basis = whole_basis(jnp.concatenate([basis_in.T, basis_out.T], axis=1))
    basis_i, basis_o = basis[:, :depth], basis[:, depth:]

    def rotated(k):
        start = ((low + k + 4) % 4) * 128
        a = lax.dynamic_slice_in_dim(activations, start, 128, 0)
        g = lax.dynamic_slice_in_dim(out_grads, start, 128, 0)
        dims = (((1,), (1,)), ((), ()))
        left = lax.dot_general(a, basis_i, dims, preferred_element_type=f32)
        right = lax.dot_general(g, basis_o, dims, preferred_element_type=f32)
        return jnp.concatenate([left, right], axis=1)

    sign = 1 - 2 * lax.axis_index("c")
    turns = (0, sign, -sign, 2)
    rows = [rotated(k) for k in turns]
    mine = reduce_step([rows[0]] + [r.astype(f16) for r in rows[1:]], 1, 2)
    quarter = [lax.dynamic_slice_in_dim(mine, ((high + k + 4) % 4) * 32, 32, 0) for k in turns]
    mine = reduce_step([quarter[0]] + [r.astype(f16) for r in quarter[1:]], 4, 8)

    position = low * 128 + high * 32 + lax.broadcasted_iota(jnp.int32, (32, 1), 0)
    counted = (position < lengths[0]).astype(bf16)
    half = mine.shape[1] // 2
    mine = mine.astype(bf16)
    mine = jnp.concatenate([mine[:, :half], mine[:, half:] * counted], axis=1)
    held = jnp.concatenate([mine, shift(mine, 4, -4), shift(mine, -4, 4), shift(mine, 8, -8)], axis=0)
    pieces = [held, shift(held, 1, -1), shift(held, -1, 1), shift(held, 2, -2)]
    statistic = 0.0
    for piece in pieces:
        statistic += lax.dot_general(
            piece[:, :half], piece[:, half:], (((0,), (0,)), ((), ())), preferred_element_type=f32
        )
    scaled = (statistic / (eigen + DAMP)).astype(bf16)
    weighted = jnp.dot(scaled, query_out, preferred_element_type=f32)
    summed = jnp.sum(weighted * query_in.astype(f32), axis=0)
    return summed.reshape(-1, RANK).sum(axis=1)[None, :]


def solution(mesh):
    fine = Mesh(mesh.devices.reshape(4, 4, 2, RING), ("y", "x", "c", "z"))
    ex = ("y", "x", "c")
    in_specs = (P(ex, "z"), P(ex, "z"), P("z", ex), P("z", ex), P(), P(ex), P(None, "z"), P(None, "z"))
    return jax.shard_map(shards, mesh=fine, in_specs=in_specs, out_specs=P(ex, "z"), check_vma=False)
```

time: 303 us -> 133 us (0.44)
  the two profiles are of different devices: /device:TPU:2 before, /device:TPU:1 now
where the time goes in v1:
time: 133 us; the launch traced here: 132 us
  starting transfers between devices  63.2 us (48%)
  waiting for transfers between devices  28.3 us (21%)
  blocking collectives  24.9 us (19%)
  matrix products  10.2 us (8%)
  other arithmetic  3.96 us (3%)
    ppermute x12, starting transfers between devices, shift(): return lax.ppermute(x, LINE, pairs)  58.3 us
    ppermute x12, waiting for transfers between devices, shift(): return lax.ppermute(x, LINE, pairs)  26.5 us
    all_to_all x1, blocking collectives, whole_basis(): lax.all_to_all(jnp.broadcast_to(columns[None], (16, kept, width)), PLANE,...  24.9 us
    ppermute x1, starting transfers between devices, whole_basis(): far = lax.ppermute(near, 'c', [(0, 1), (1, 0)])  4.87 us
    dot_general x4, matrix products, rotated(): right = lax.dot_general(g, basis_o, dims, preferred_element_type=f32)  3.17 us
    dot_general x3, matrix products, shards(): lax.dot_general(piece[:, :half], piece[:, half:], (((0,), (0,)), ((), ())...  2.93 us
    dot_general x1, matrix products, shards(): weighted = jnp.dot(scaled, query_out, preferred_element_type=f32)  2.87 us
  transfers between devices with their start and end apart: 13, of which 8 were waited for; matrix products, arithmetic and copies ran while one was open for 2% of the time, Pallas kernels for 0%

profile of v1, /device:TPU:1, one launch (start us, length us, event | category | flops | bytes accessed | tf_op | source)
XLA Modules:
  0.0 132.1 jit_solution(9569013210843240351)
XLA Ops:
  0.0 1.0 pad_maximum_fusion.5
  1.1 24.9 %all_to_all.5 = bf16[16,16,2360]{2,1,0:T(8,128)(2,1)S(1)} all-to-all(bf16[16,16,2360]{2,1,0:T(8,128)(2,1)S(1)} %broadcast_in_dim.4), channel_id=1, replica_groups=mesh['y'=4,'x'=4,'c'=2,'z'=16] {'y','x'}, dimensions={0} | all-to-all | bytes 2416640 | tf_op jit(solution)/shard_map/all_to_all | solution.py:24
  26.0 4.9 %collective-permute-start = (bf16[16,16,2360]{2,1,0:T(8,128)(2,1)S(1)}, bf16[16,16,2360]{2,1,0:T(8,128)(2,1)}, u32[]{:S(2)}, u32[]{:S(2)}) collective-permute-start(bf16[16,16,2360]{2,1,0:T(8,128)(2,1)S(1)} %all_to_all.5), channel_id=1, source_target_pairs={{0,16},{16,0},{1,17},{17,1},{2,18},{18,2},{3,19},{19,3},{4,20},{20... | collective-permute-start | bytes 3624968 | tf_op jit(solution)/shard_map/ppermute | solution.py:25
  31.7 1.9 %collective-permute-done = bf16[16,16,2360]{2,1,0:T(8,128)(2,1)} collective-permute-done((bf16[16,16,2360]{2,1,0:T(8,128)(2,1)S(1)}, bf16[16,16,2360]{2,1,0:T(8,128)(2,1)}, u32[]{:S(2)}, u32[]{:S(2)}) %collective-permute-start) | collective-permute-done | bytes 1208352 | tf_op jit(solution)/shard_map/ppermute | solution.py:25
  33.5 1.6 %select_bitcast_fusion.1 = (bf16[16,1,16,2360]{3,2,1,0:T(8,128)(2,1)S(1)}, bf16[16,1,16,2360]{3,2,1,0:T(8,128)(2,1)S(1)}) fusion(bf16[16,16,2360]{2,1,0:T(8,128)(2,1)S(1)} %all_to_all.5, bf16[16,16,2360]{2,1,0:T(8,128)(2,1)} %collective-permute-done, pred[]{:T(512)S(6)} %eq.13), kind=kLoop, calls=%fused_computation.16 | loop fusion | flops 1208320 | bytes 4833281 | tf_op jit(solution)/shard_map/stack | solution.py:27
  35.4 0.8 fusion.19
  36.7 0.8 fusion.16
  37.8 0.8 fusion.13
  39.0 11.3 %collective-permute-start.3 = (f16[128,1024]{1,0:T(8,128)(2,1)S(1)}, f16[128,1024]{1,0:T(8,128)(2,1)S(1)}, u32[]{:S(2)}, u32[]{:S(2)}) collective-permute-start(f16[128,1024]{1,0:T(8,128)(2,1)S(1)} %pad_maximum_fusion.3), channel_id=1, source_target_pairs={{0,2},{1,3},{2,4},{3,5},{4,6},{5,7},{6,8},{7,9},{8,10},{9,11},{10,... | collective-permute-start | bytes 786440 | tf_op jit(solution)/shard_map/ppermute | solution.py:19
  50.4 2.6 %collective-permute-start.2 = (f16[128,1024]{1,0:T(8,128)(2,1)S(1)}, f16[128,1024]{1,0:T(8,128)(2,1)S(1)}, u32[]{:S(2)}, u32[]{:S(2)}) collective-permute-start(f16[128,1024]{1,0:T(8,128)(2,1)S(1)} %pad_maximum_fusion.2), channel_id=1, source_target_pairs={{0,15},{1,0},{2,1},{3,2},{4,3},{5,4},{6,5},{7,6},{8,7},{9,8},{10,9... | collective-permute-start | bytes 786440 | tf_op jit(solution)/shard_map/ppermute | solution.py:19
  53.1 3.9 %collective-permute-start.1 = (f16[128,1024]{1,0:T(8,128)(2,1)S(1)}, f16[128,1024]{1,0:T(8,128)(2,1)S(1)}, u32[]{:S(2)}, u32[]{:S(2)}) collective-permute-start(f16[128,1024]{1,0:T(8,128)(2,1)S(1)} %pad_maximum_fusion.1), channel_id=1, source_target_pairs={{0,1},{1,2},{2,3},{3,4},{4,5},{5,6},{6,7},{7,8},{8,9},{9,10},{10,1... | collective-permute-start | bytes 786440 | tf_op jit(solution)/shard_map/ppermute | solution.py:19
  57.0 0.8 fusion.10
  58.1 3.1 %collective-permute-done.2 = f16[128,1024]{1,0:T(8,128)(2,1)S(1)} collective-permute-done((f16[128,1024]{1,0:T(8,128)(2,1)S(1)}, f16[128,1024]{1,0:T(8,128)(2,1)S(1)}, u32[]{:S(2)}, u32[]{:S(2)}) %collective-permute-start.2) | collective-permute-done | bytes 262176 | tf_op jit(solution)/shard_map/ppermute | solution.py:19
  61.2 0.8 collective-permute-done.1
  62.3 8.3 %collective-permute-start.6 = (f16[32,1024]{1,0:T(8,128)(2,1)S(1)}, f16[32,1024]{1,0:T(8,128)(2,1)S(1)}, u32[]{:S(2)}, u32[]{:S(2)}) collective-permute-start(f16[32,1024]{1,0:T(8,128)(2,1)S(1)} %get-tuple-element.8), channel_id=1, source_target_pairs={{0,8},{1,9},{2,10},{3,11},{4,12},{5,13},{6,14},{7,15},{8,0},{9,1},... | collective-permute-start | bytes 196616 | tf_op jit(solution)/shard_map/ppermute | solution.py:19
  70.6 4.8 %collective-permute-start.5 = (f16[32,1024]{1,0:T(8,128)(2,1)S(1)}, f16[32,1024]{1,0:T(8,128)(2,1)S(1)}, u32[]{:S(2)}, u32[]{:S(2)}) collective-permute-start(f16[32,1024]{1,0:T(8,128)(2,1)S(1)} %get-tuple-element.9), channel_id=1, source_target_pairs={{0,12},{1,13},{2,14},{3,15},{4,0},{5,1},{6,2},{7,3},{8,4},{9,5},{1... | collective-permute-start | bytes 196616 | tf_op jit(solution)/shard_map/ppermute | solution.py:19
  75.4 4.4 %collective-permute-start.4 = (f16[32,1024]{1,0:T(8,128)(2,1)S(1)}, f16[32,1024]{1,0:T(8,128)(2,1)S(1)}, u32[]{:S(2)}, u32[]{:S(2)}) collective-permute-start(f16[32,1024]{1,0:T(8,128)(2,1)S(1)} %get-tuple-element.7), channel_id=1, source_target_pairs={{0,4},{1,5},{2,6},{3,7},{4,8},{5,9},{6,10},{7,11},{8,12},{9,13},{1... | collective-permute-start | bytes 196616 | tf_op jit(solution)/shard_map/ppermute | solution.py:19
  79.8 7.4 %collective-permute-done.4 = f16[32,1024]{1,0:T(8,128)(2,1)S(1)} collective-permute-done((f16[32,1024]{1,0:T(8,128)(2,1)S(1)}, f16[32,1024]{1,0:T(8,128)(2,1)S(1)}, u32[]{:S(2)}, u32[]{:S(2)}) %collective-permute-start.4) | collective-permute-done | bytes 65568 | tf_op jit(solution)/shard_map/ppermute | solution.py:19
  87.3 4.2 %collective-permute-start.9 = (bf16[32,1024]{1,0:T(8,128)(2,1)S(1)}, bf16[32,1024]{1,0:T(8,128)(2,1)S(1)}, u32[]{:S(2)}, u32[]{:S(2)}) collective-permute-start(bf16[32,1024]{1,0:T(8,128)(2,1)S(1)} %pad_maximum_fusion.6), channel_id=1, source_target_pairs={{0,8},{1,9},{2,10},{3,11},{4,12},{5,13},{6,14},{7,15},{8,0},{9,1},... | collective-permute-start | bytes 196616 | tf_op jit(solution)/shard_map/ppermute | solution.py:19
  91.5 6.9 %collective-permute-start.8 = (bf16[32,1024]{1,0:T(8,128)(2,1)S(1)}, bf16[32,1024]{1,0:T(8,128)(2,1)S(1)}, u32[]{:S(2)}, u32[]{:S(2)}) collective-permute-start(bf16[32,1024]{1,0:T(8,128)(2,1)S(1)} %pad_maximum_fusion.6), channel_id=1, source_target_pairs={{0,12},{1,13},{2,14},{3,15},{4,0},{5,1},{6,2},{7,3},{8,4},{9,5},{1... | collective-permute-start | bytes 196616 | tf_op jit(solution)/shard_map/ppermute | solution.py:19
  98.4 2.3 %collective-permute-start.7 = (bf16[32,1024]{1,0:T(8,128)(2,1)S(1)}, bf16[32,1024]{1,0:T(8,128)(2,1)S(1)}, u32[]{:S(2)}, u32[]{:S(2)}) collective-permute-start(bf16[32,1024]{1,0:T(8,128)(2,1)S(1)} %pad_maximum_fusion.6), channel_id=1, source_target_pairs={{0,4},{1,5},{2,6},{3,7},{4,8},{5,9},{6,10},{7,11},{8,12},{9,13},{1... | collective-permute-start | bytes 196616 | tf_op jit(solution)/shard_map/ppermute | solution.py:19
  100.7 1.5 %collective-permute-done.9 = bf16[32,1024]{1,0:T(8,128)(2,1)S(1)} collective-permute-done((bf16[32,1024]{1,0:T(8,128)(2,1)S(1)}, bf16[32,1024]{1,0:T(8,128)(2,1)S(1)}, u32[]{:S(2)}, u32[]{:S(2)}) %collective-permute-start.9) | collective-permute-done | bytes 65568 | tf_op jit(solution)/shard_map/ppermute | solution.py:19
  102.2 2.7 %collective-permute-done.8 = bf16[32,1024]{1,0:T(8,128)(2,1)S(1)} collective-permute-done((bf16[32,1024]{1,0:T(8,128)(2,1)S(1)}, bf16[32,1024]{1,0:T(8,128)(2,1)S(1)}, u32[]{:S(2)}, u32[]{:S(2)}) %collective-permute-start.8) | collective-permute-done | bytes 65568 | tf_op jit(solution)/shard_map/ppermute | solution.py:19
  104.9 4.7 %collective-permute-done.7 = bf16[32,1024]{1,0:T(8,128)(2,1)S(1)} collective-permute-done((bf16[32,1024]{1,0:T(8,128)(2,1)S(1)}, bf16[32,1024]{1,0:T(8,128)(2,1)S(1)}, u32[]{:S(2)}, u32[]{:S(2)}) %collective-permute-start.7) | collective-permute-done | bytes 65568 | tf_op jit(solution)/shard_map/ppermute | solution.py:19
  109.7 3.2 %collective-permute-start.12 = (bf16[128,1024]{1,0:T(8,128)(2,1)S(1)}, bf16[128,1024]{1,0:T(8,128)(2,1)S(1)}, u32[]{:S(2)}, u32[]{:S(2)}) collective-permute-start(bf16[128,1024]{1,0:T(8,128)(2,1)S(1)} %pad_maximum_fusion.4), channel_id=1, source_target_pairs={{0,2},{1,3},{2,4},{3,5},{4,6},{5,7},{6,8},{7,9},{8,10},{9,11},{10,... | collective-permute-start | bytes 786440 | tf_op jit(solution)/shard_map/ppermute | solution.py:19
  112.8 3.9 %collective-permute-start.11 = (bf16[128,1024]{1,0:T(8,128)(2,1)S(1)}, bf16[128,1024]{1,0:T(8,128)(2,1)S(1)}, u32[]{:S(2)}, u32[]{:S(2)}) collective-permute-start(bf16[128,1024]{1,0:T(8,128)(2,1)S(1)} %pad_maximum_fusion.4), channel_id=1, source_target_pairs={{0,15},{1,0},{2,1},{3,2},{4,3},{5,4},{6,5},{7,6},{8,7},{9,8},{10,9... | collective-permute-start | bytes 786440 | tf_op jit(solution)/shard_map/ppermute | solution.py:19
  116.7 2.6 %collective-permute-start.10 = (bf16[128,1024]{1,0:T(8,128)(2,1)S(1)}, bf16[128,1024]{1,0:T(8,128)(2,1)S(1)}, u32[]{:S(2)}, u32[]{:S(2)}) collective-permute-start(bf16[128,1024]{1,0:T(8,128)(2,1)S(1)} %pad_maximum_fusion.4), channel_id=1, source_target_pairs={{0,1},{1,2},{2,3},{3,4},{4,5},{5,6},{6,7},{7,8},{8,9},{9,10},{10,1... | collective-permute-start | bytes 786440 | tf_op jit(solution)/shard_map/ppermute | solution.py:19
  119.7 6.2 %collective-permute-done.11 = bf16[128,1024]{1,0:T(8,128)(2,1)S(1)} collective-permute-done((bf16[128,1024]{1,0:T(8,128)(2,1)S(1)}, bf16[128,1024]{1,0:T(8,128)(2,1)S(1)}, u32[]{:S(2)}, u32[]{:S(2)}) %collective-permute-start.11) | collective-permute-done | bytes 262176 | tf_op jit(solution)/shard_map/ppermute | solution.py:19
  125.8 1.3 fusion.37
  127.1 1.3 fusion.40
  128.5 2.9 %fusion.12 = f32[512]{0:T(512)S(1)} fusion(bf16[512,512]{1,0:T(8,128)(2,1)} %param.15, bf16[512,512]{1,0:T(8,128)(2,1)} %param.14, f32[512,512]{1,0:T(8,128)S(1)} %fusion.34, f32[512,512]{1,0:T(8,128)} %fusion.37, f32[512,512]{1,0:T(8,128)} %fusion.40, f32[512,512]{1,0:T(8,128)} %param.12, bf16[128,1024]{1,0:T(8,128)(2,1)S(1)} %pad_maximum_fusion.4), kind=kOutput, calls=%fused_computation.17 | convolution fusion | flops 337903104 | bytes 5507072 | tf_op jit(solution)/shard_map/dot_general | solution.py:77
  131.4 0.6 reduce_sum.19
  (27 shorter events, 2.8 us)
Async XLA Ops:
  0.0 35.4 %copy-start = (bf16[512,1848]{0,1:T(8,128)(2,1)S(1)}, bf16[512,1848]{0,1:T(8,128)(2,1)}, u32[]{:S(2)}) copy-start(bf16[512,1848]{0,1:T(8,128)(2,1)} %param.9) | copy-start | bytes 5677060
  26.0 7.6 %collective-permute-start = (bf16[16,16,2360]{2,1,0:T(8,128)(2,1)S(1)}, bf16[16,16,2360]{2,1,0:T(8,128)(2,1)}, u32[]{:S(2)}, u32[]{:S(2)}) collective-permute-start(bf16[16,16,2360]{2,1,0:T(8,128)(2,1)S(1)} %all_to_all.5), channel_id=1, source_target_pairs={{0,16},{16,0},{1,17},{17,1},{2,18},{18,2},{3,19},{19,3},{4,20},{20... | collective-permute-start | bytes 3624968 | tf_op jit(solution)/shard_map/ppermute | solution.py:25
  35.4 1.0 copy-start.1
  39.0 19.1 %collective-permute-start.3 = (f16[128,1024]{1,0:T(8,128)(2,1)S(1)}, f16[128,1024]{1,0:T(8,128)(2,1)S(1)}, u32[]{:S(2)}, u32[]{:S(2)}) collective-permute-start(f16[128,1024]{1,0:T(8,128)(2,1)S(1)} %pad_maximum_fusion.3), channel_id=1, source_target_pairs={{0,2},{1,3},{2,4},{3,5},{4,6},{5,7},{6,8},{7,9},{8,10},{9,11},{10,... | collective-permute-start | bytes 786440 | tf_op jit(solution)/shard_map/ppermute | solution.py:19
  50.4 10.8 %collective-permute-start.2 = (f16[128,1024]{1,0:T(8,128)(2,1)S(1)}, f16[128,1024]{1,0:T(8,128)(2,1)S(1)}, u32[]{:S(2)}, u32[]{:S(2)}) collective-permute-start(f16[128,1024]{1,0:T(8,128)(2,1)S(1)} %pad_maximum_fusion.2), channel_id=1, source_target_pairs={{0,15},{1,0},{2,1},{3,2},{4,3},{5,4},{6,5},{7,6},{8,7},{9,8},{10,9... | collective-permute-start | bytes 786440 | tf_op jit(solution)/shard_map/ppermute | solution.py:19
  53.1 8.9 %collective-permute-start.1 = (f16[128,1024]{1,0:T(8,128)(2,1)S(1)}, f16[128,1024]{1,0:T(8,128)(2,1)S(1)}, u32[]{:S(2)}, u32[]{:S(2)}) collective-permute-start(f16[128,1024]{1,0:T(8,128)(2,1)S(1)} %pad_maximum_fusion.1), channel_id=1, source_target_pairs={{0,1},{1,2},{2,3},{3,4},{4,5},{5,6},{6,7},{7,8},{8,9},{9,10},{10,1... | collective-permute-start | bytes 786440 | tf_op jit(solution)/shard_map/ppermute | solution.py:19
  62.3 17.5 %collective-permute-start.6 = (f16[32,1024]{1,0:T(8,128)(2,1)S(1)}, f16[32,1024]{1,0:T(8,128)(2,1)S(1)}, u32[]{:S(2)}, u32[]{:S(2)}) collective-permute-start(f16[32,1024]{1,0:T(8,128)(2,1)S(1)} %get-tuple-element.8), channel_id=1, source_target_pairs={{0,8},{1,9},{2,10},{3,11},{4,12},{5,13},{6,14},{7,15},{8,0},{9,1},... | collective-permute-start | bytes 196616 | tf_op jit(solution)/shard_map/ppermute | solution.py:19
  70.6 9.2 %collective-permute-start.5 = (f16[32,1024]{1,0:T(8,128)(2,1)S(1)}, f16[32,1024]{1,0:T(8,128)(2,1)S(1)}, u32[]{:S(2)}, u32[]{:S(2)}) collective-permute-start(f16[32,1024]{1,0:T(8,128)(2,1)S(1)} %get-tuple-element.9), channel_id=1, source_target_pairs={{0,12},{1,13},{2,14},{3,15},{4,0},{5,1},{6,2},{7,3},{8,4},{9,5},{1... | collective-permute-start | bytes 196616 | tf_op jit(solution)/shard_map/ppermute | solution.py:19
  75.4 11.8 %collective-permute-start.4 = (f16[32,1024]{1,0:T(8,128)(2,1)S(1)}, f16[32,1024]{1,0:T(8,128)(2,1)S(1)}, u32[]{:S(2)}, u32[]{:S(2)}) collective-permute-start(f16[32,1024]{1,0:T(8,128)(2,1)S(1)} %get-tuple-element.7), channel_id=1, source_target_pairs={{0,4},{1,5},{2,6},{3,7},{4,8},{5,9},{6,10},{7,11},{8,12},{9,13},{1... | collective-permute-start | bytes 196616 | tf_op jit(solution)/shard_map/ppermute | solution.py:19
  87.3 14.9 %collective-permute-start.9 = (bf16[32,1024]{1,0:T(8,128)(2,1)S(1)}, bf16[32,1024]{1,0:T(8,128)(2,1)S(1)}, u32[]{:S(2)}, u32[]{:S(2)}) collective-permute-start(bf16[32,1024]{1,0:T(8,128)(2,1)S(1)} %pad_maximum_fusion.6), channel_id=1, source_target_pairs={{0,8},{1,9},{2,10},{3,11},{4,12},{5,13},{6,14},{7,15},{8,0},{9,1},... | collective-permute-start | bytes 196616 | tf_op jit(solution)/shard_map/ppermute | solution.py:19
  91.5 13.5 %collective-permute-start.8 = (bf16[32,1024]{1,0:T(8,128)(2,1)S(1)}, bf16[32,1024]{1,0:T(8,128)(2,1)S(1)}, u32[]{:S(2)}, u32[]{:S(2)}) collective-permute-start(bf16[32,1024]{1,0:T(8,128)(2,1)S(1)} %pad_maximum_fusion.6), channel_id=1, source_target_pairs={{0,12},{1,13},{2,14},{3,15},{4,0},{5,1},{6,2},{7,3},{8,4},{9,5},{1... | collective-permute-start | bytes 196616 | tf_op jit(solution)/shard_map/ppermute | solution.py:19
  98.4 11.2 %collective-permute-start.7 = (bf16[32,1024]{1,0:T(8,128)(2,1)S(1)}, bf16[32,1024]{1,0:T(8,128)(2,1)S(1)}, u32[]{:S(2)}, u32[]{:S(2)}) collective-permute-start(bf16[32,1024]{1,0:T(8,128)(2,1)S(1)} %pad_maximum_fusion.6), channel_id=1, source_target_pairs={{0,4},{1,5},{2,6},{3,7},{4,8},{5,9},{6,10},{7,11},{8,12},{9,13},{1... | collective-permute-start | bytes 196616 | tf_op jit(solution)/shard_map/ppermute | solution.py:19
  109.7 9.7 %collective-permute-start.12 = (bf16[128,1024]{1,0:T(8,128)(2,1)S(1)}, bf16[128,1024]{1,0:T(8,128)(2,1)S(1)}, u32[]{:S(2)}, u32[]{:S(2)}) collective-permute-start(bf16[128,1024]{1,0:T(8,128)(2,1)S(1)} %pad_maximum_fusion.4), channel_id=1, source_target_pairs={{0,2},{1,3},{2,4},{3,5},{4,6},{5,7},{6,8},{7,9},{8,10},{9,11},{10,... | collective-permute-start | bytes 786440 | tf_op jit(solution)/shard_map/ppermute | solution.py:19
  112.8 13.0 %collective-permute-start.11 = (bf16[128,1024]{1,0:T(8,128)(2,1)S(1)}, bf16[128,1024]{1,0:T(8,128)(2,1)S(1)}, u32[]{:S(2)}, u32[]{:S(2)}) collective-permute-start(bf16[128,1024]{1,0:T(8,128)(2,1)S(1)} %pad_maximum_fusion.4), channel_id=1, source_target_pairs={{0,15},{1,0},{2,1},{3,2},{4,3},{5,4},{6,5},{7,6},{8,7},{9,8},{10,9... | collective-permute-start | bytes 786440 | tf_op jit(solution)/shard_map/ppermute | solution.py:19
  116.7 10.5 %collective-permute-start.10 = (bf16[128,1024]{1,0:T(8,128)(2,1)S(1)}, bf16[128,1024]{1,0:T(8,128)(2,1)S(1)}, u32[]{:S(2)}, u32[]{:S(2)}) collective-permute-start(bf16[128,1024]{1,0:T(8,128)(2,1)S(1)} %pad_maximum_fusion.4), channel_id=1, source_target_pairs={{0,1},{1,2},{2,3},{3,4},{4,5},{5,6},{6,7},{7,8},{8,9},{9,10},{10,1... | collective-permute-start | bytes 786440 | tf_op jit(solution)/shard_map/ppermute | solution.py:19

commit v2 on v0

v2 whole, which is shorter than its diff:
```python
import jax
import jax.numpy as jnp
from jax import lax
from jax.sharding import Mesh
from jax.sharding import PartitionSpec as P

RANK = 8
DAMP = 0.1
UP_IN = 16.0
UP_OUT = 8.0
LIFT_IN = 2.0**19
LIFT_OUT = 2.0**20


def rotate(rows, columns):
    return lax.dot_general(rows, columns, (((1,), (1,)), ((), ())), preferred_element_type=jnp.float32)


def shards(activations, out_grads, basis_in, basis_out, eigen, lengths, query_in, query_out):
    f32, bf16, f16 = jnp.float32, jnp.bfloat16, jnp.float16
    depth = basis_in.shape[0]
    lifted = [basis_in.T.astype(f32) * LIFT_IN, basis_out.T.astype(f32) * LIFT_OUT]
    own = jnp.concatenate(lifted, axis=1).astype(f16)
    basis = lax.all_gather(own, ("y", "x", "c"), axis=0, tiled=True).astype(bf16)
    low_in, low_out = UP_IN / LIFT_IN, UP_OUT / LIFT_OUT
    left = rotate(activations, basis[:, :depth]) * low_in
    right = rotate(out_grads, basis[:, depth:]) * low_out
    partial = jnp.concatenate([left.astype(f16), right.astype(f16)], axis=1)
    rotated = lax.psum(partial, "z").astype(f32)
    half = rotated.shape[1] // 2
    position = lax.broadcasted_iota(jnp.int32, (rotated.shape[0], 1), 0)
    counted = (position < lengths[0]).astype(f32)
    inputs = (rotated[:, :half] * (1 / UP_IN)).astype(bf16)
    outputs = (rotated[:, half:] * (counted * (1 / UP_OUT))).astype(bf16)
    statistic = lax.dot_general(inputs, outputs, (((0,), (0,)), ((), ())), preferred_element_type=f32)
    scaled = (statistic / (eigen + DAMP)).astype(bf16)
    weighted = jnp.dot(scaled, query_out, preferred_element_type=f32)
    summed = jnp.sum(weighted * query_in.astype(f32), axis=0)
    return summed.reshape(-1, RANK).sum(axis=1)[None, :]


def solution(mesh):
    fine = Mesh(mesh.devices.reshape(4, 4, 2, 16), ("y", "x", "c", "z"))
    ex = ("y", "x", "c")
    in_specs = (P(ex, "z"), P(ex, "z"), P("z", ex), P("z", ex), P(), P(ex), P(None, "z"), P(None, "z"))
    return jax.shard_map(shards, mesh=fine, in_specs=in_specs, out_specs=P(ex, "z"), check_vma=False)
```

time: 303 us -> 114 us (0.38)
  waiting for transfers between devices: 247 us -> 0 us
  blocking collectives: 27.7 us -> 102 us
  between operations: 13.9 us -> 0.73 us
  other arithmetic: 2.1 us -> 5.58 us
  local copies, waits for them, and re-layouts: 4.12 us -> 0.81 us
  matrix products: 7.63 us -> 4.48 us
    psum x1 -> x0, waiting for transfers between devices: 137 us -> none  [shards(): lax.psum(rotated_block(shares, offset, seq_length, split_at), 'tp')]
    unnamed x4 -> x0, waiting for transfers between devices: 73.2 us -> none
    psum x0 -> x1, blocking collectives: none -> 72.9 us  [shards(): rotated = lax.psum(partial, 'z').astype(f32)]
    all_gather x1 -> x0, waiting for transfers between devices: 37.1 us -> none  [shards(): lax.all_gather(basis_out, 'ex', axis=1, tiled=True)]
    unnamed x6, local copies, waits for them, and re-layouts: 4.03 us -> 0.73 us
    dot_general x4 -> x3, matrix products: 7.63 us -> 4.48 us  [the longest x1 2.76 us: shards(): weighted = jnp.dot(scaled, query_out, preferred_element_type=f32)]
  transfers between devices with their start and end apart: 3 -> 0, of which waited for: 3 -> 0; matrix products, arithmetic and copies ran while one was open for 0% -> 0% of each run, Pallas kernels for 0% -> 0%
where the time goes in v2:
time: 114 us
  blocking collectives  102 us (89%)
  other arithmetic  5.58 us (5%)
  matrix products  4.48 us (4%)
    psum x1, blocking collectives, shards(): rotated = lax.psum(partial, 'z').astype(f32)  72.9 us
    all_gather x1, blocking collectives, shards(): lax.all_gather(own, ('y', 'x', 'c'), axis=0, tiled=True).astype(bf16)  29.3 us
    dot_general x1, matrix products, shards(): weighted = jnp.dot(scaled, query_out, preferred_element_type=f32)  2.76 us

profile of v2, /device:TPU:2, one launch (start us, length us, event | category | flops | bytes accessed | tf_op | source)
XLA Modules:
  0.0 113.8 jit_solution(13291656960972981214)
XLA Ops:
  0.0 0.0 copy-start
  0.0 1.0 fusion.27
  1.0 0.7 fusion.28
  1.7 29.3 %all-gather.1 = f16[512,2360]{1,0:T(8,128)(2,1)S(1)} all-gather(f16[16,2360]{1,0:T(8,128)(2,1)S(1)} %pad_maximum_fusion.1), channel_id=1, replica_groups=mesh['y'=4,'x'=4,'c'=2,'z'=16] {'y','x','c'}, dimensions={0}, use_global_device_ids=true | all-gather | bytes 2492160 | tf_op jit(solution)/shard_map/all_gather | solution.py:24
  31.1 0.0 copy-start.1
  31.1 0.3 convert_element_type.42
  31.4 0.7 copy-done.1
  32.1 0.5 fusion.11
  32.6 0.0 copy-done
  32.6 1.3 %fusion.12 = f16[512,512]{0,1:T(8,128)(2,1)S(1)} fusion(bf16[512,1848]{0,1:T(8,128)(2,1)S(1)} %copy-done, bf16[512,2360]{1,0:T(8,128)(2,1)S(1)} %convert_element_type.42), kind=kOutput, calls=%fused_computation.11 | convolution fusion | flops 969408512 | bytes 4382720 | tf_op jit(solution)/shard_map/dot_general | solution.py:16
  33.8 1.2 %pad_maximum_fusion = f16[512,1024]{0,1:T(8,128)(2,1)} fusion(f16[512,512]{0,1:T(8,128)(2,1)S(1)} %fusion.12, f16[512,512]{0,1:T(8,128)(2,1)S(1)} %fusion.11), kind=kLoop, calls=%fused_computation.16 | loop fusion | flops 524288 | bytes 2097152 | tf_op jit(solution)/shard_map/concatenate | solution.py:28
  35.1 72.9 %all-reduce.1 = u32[65536,4]{0,1:T(4,128)S(1)} all-reduce(u32[65536,4]{0,1:T(4,128)} %bitcast.17), channel_id=1, replica_groups=mesh['y'=4,'x'=4,'c'=2,'z'=16] {'z'}, use_global_device_ids=true, to_apply=%region_0.0.clone | all-reduce | flops 262144 | bytes 2097152 | tf_op jit(solution)/shard_map/psum | solution.py:29
  108.0 0.0 copy-start.2
  108.0 1.6 %convert_element_type.47 = f32[512,1024]{0,1:T(8,128)} convert(f16[512,1024]{0,1:T(8,128)(2,1)S(1)} %bitcast.16) | non-fusion elementwise | flops 524288 | bytes 3145728 | tf_op jit(solution)/shard_map/convert_element_type | solution.py:29
  110.3 0.0 copy-done.2
  110.3 2.8 %fusion.10 = f32[512]{0:T(512)S(1)} fusion(bf16[512,512]{1,0:T(8,128)(2,1)S(1)} %copy-done.2, bf16[512,512]{1,0:T(8,128)(2,1)} %param.14, f32[512,512]{1,0:T(8,128)} %param.12, f32[512,1024]{0,1:T(8,128)} %convert_element_type.47, f32[512]{0:T(512)S(1)} %fusion.29), kind=kOutput, calls=%fused_computation.9 | convolution fusion | flops 539491840 | bytes 4198400 | tf_op jit(solution)/shard_map/dot_general | solution.py:37
  113.1 0.1 reshape.10
  113.2 0.6 reduce_sum.19
  (2 shorter events, 0.0 us)
Async XLA Ops:
  0.0 32.6 %copy-start = (bf16[512,1848]{0,1:T(8,128)(2,1)S(1)}, bf16[512,1848]{0,1:T(8,128)(2,1)}, u32[]{:S(2)}) copy-start(bf16[512,1848]{0,1:T(8,128)(2,1)} %param.9) | copy-start | bytes 5677060
  31.1 1.0 copy-start.1
  108.0 2.3 %copy-start.2 = (bf16[512,512]{1,0:T(8,128)(2,1)S(1)}, bf16[512,512]{1,0:T(8,128)(2,1)}, u32[]{:S(2)}) copy-start(bf16[512,512]{1,0:T(8,128)(2,1)} %param.15) | copy-start | bytes 1572868

commit v3 on v2

v3 whole, which is shorter than its diff:
```python
import jax
import jax.numpy as jnp
from jax import lax
from jax.sharding import Mesh
from jax.sharding import PartitionSpec as P

RANK = 8
DAMP = 0.1
UP_IN = 16.0
UP_OUT = 8.0
LIFT = 2.0**19


def rotate(rows, columns):
    return lax.dot_general(rows, columns, (((1,), (1,)), ((), ())), preferred_element_type=jnp.float32)


def shards(activations, out_grads, basis_in, basis_out, eigen, lengths, query_in, query_out):
    f32, bf16, f16 = jnp.float32, jnp.bfloat16, jnp.float16
    depth = basis_in.shape[0]
    own = jnp.concatenate([basis_in.T, basis_out.T], axis=1)
    own = (own.astype(f32) * LIFT).astype(f16)
    basis = lax.all_gather(own, ("y", "x", "c"), axis=0, tiled=True).astype(bf16)
    right = (rotate(out_grads, basis[:, depth:]) * (UP_OUT / LIFT)).astype(f16)
    basis, right = lax.optimization_barrier((basis, right))
    left = (rotate(activations, basis[:, :depth]) * (UP_IN / LIFT)).astype(f16)
    left, right = lax.psum((left, right), "z")
    position = lax.broadcasted_iota(jnp.int32, (right.shape[0], 1), 0)
    counted = (position < lengths[0]).astype(f32)
    inputs = (left.astype(f32) * (1 / UP_IN)).astype(bf16)
    outputs = (right.astype(f32) * (counted * (1 / UP_OUT))).astype(bf16)
    statistic = lax.dot_general(inputs, outputs, (((0,), (0,)), ((), ())), preferred_element_type=f32)
    scaled = (statistic / (eigen + DAMP)).astype(bf16)
    weighted = jnp.dot(scaled, query_out, preferred_element_type=f32)
    summed = jnp.sum(weighted * query_in.astype(f32), axis=0)
    return summed.reshape(-1, RANK).sum(axis=1)[None, :]


def solution(mesh):
    fine = Mesh(mesh.devices.reshape(4, 4, 2, 16), ("y", "x", "c", "z"))
    ex = ("y", "x", "c")
    in_specs = (P(ex, "z"), P(ex, "z"), P("z", ex), P("z", ex), P(), P(ex), P(None, "z"), P(None, "z"))
    return jax.shard_map(shards, mesh=fine, in_specs=in_specs, out_specs=P(ex, "z"), check_vma=False)
```

time: 114 us -> 109 us (0.956)
  other arithmetic: 5.58 us -> 1.95 us
    mul x3 -> x1, other arithmetic: 1.71 us -> 0.01 us  [shards(): outputs = (right.astype(f32) * (counted * (1 / UP_OUT))).astype(bf16)]
    concatenate x2 -> x0, other arithmetic: 1.27 us -> none  [the longest x1 1.24 us: shards(): partial = jnp.concatenate([left.astype(f16), right.astype(f16)], axis=1)]
where the time goes in v3:
time: 109 us
  blocking collectives  102 us (94%)
  matrix products  4.16 us (4%)
  other arithmetic  1.95 us (2%)
    psum x1, blocking collectives, shards(): left, right = lax.psum((left, right), 'z')  72.9 us
    all_gather x1, blocking collectives, shards(): lax.all_gather(own, ('y', 'x', 'c'), axis=0, tiled=True).astype(bf16)  29.3 us
    dot_general x1, matrix products, shards(): weighted = jnp.dot(scaled, query_out, preferred_element_type=f32)  2.44 us

profile of v3, /device:TPU:2, one launch (start us, length us, event | category | flops | bytes accessed | tf_op | source)
XLA Modules:
  0.0 109.2 jit_solution(5116912374459370407)
XLA Ops:
  0.0 0.0 copy-start
  0.0 1.0 multiply_convert_fusion.6
  1.0 29.3 %all-gather.1 = f16[512,2360]{1,0:T(8,128)(2,1)S(1)} all-gather(f16[16,2360]{1,0:T(8,128)(2,1)S(1)} %multiply_convert_fusion.6), channel_id=1, replica_groups=mesh['y'=4,'x'=4,'c'=2,'z'=16] {'y','x','c'}, dimensions={0}, use_global_device_ids=true | all-gather | bytes 2492160 | tf_op jit(solution)/shard_map/all_gather | solution.py:23
  30.3 0.3 convert_element_type.42
  30.6 0.0 copy-done
  30.6 0.0 copy-start.1
  30.7 1.3 %fusion.11 = f16[512,512]{0,1:T(8,128)(2,1)S(1)} fusion(bf16[512,1848]{0,1:T(8,128)(2,1)S(1)} %copy-done, bf16[512,2360]{1,0:T(8,128)(2,1)S(1)} %convert_element_type.42), kind=kOutput, calls=%fused_computation.10 | convolution fusion | flops 969408512 | bytes 4382720 | tf_op jit(solution)/shard_map/dot_general | solution.py:15
  31.9 0.0 copy-done.1
  31.9 0.0 copy-start.2
  31.9 0.5 fusion.5
  32.4 72.9 %all-reduce.2 = (u32[32768,4]{0,1:T(4,128)}, u32[32768,4]{0,1:T(4,128)}) all-reduce(u32[32768,4]{0,1:T(4,128)S(1)} %bitcast.18, u32[32768,4]{0,1:T(4,128)S(1)} %bitcast.17), channel_id=1, replica_groups=mesh['y'=4,'x'=4,'c'=2,'z'=16] {'z'}, use_global_device_ids=true, to_apply=%region_0.0.clone | all-reduce | flops 262144 | bytes 2097152 | tf_op jit(solution)/shard_map/psum | solution.py:27
  106.0 0.0 copy-done.2
  106.0 2.4 %fusion.10 = f32[512]{0:T(512)S(1)} fusion(bf16[512,512]{1,0:T(8,128)(2,1)S(1)} %copy-done.2, bf16[512,512]{1,0:T(8,128)(2,1)} %param.14, f32[512,512]{1,0:T(8,128)} %param.12, f16[512,512]{0,1:T(8,128)(2,1)} %bitcast.21, f16[512,512]{0,1:T(8,128)(2,1)} %bitcast.22, f32[512]{0:T(512)S(1)} %fusion.20), kind=kOutput, calls=%fused_computation.9 | convolution fusion | flops 540016128 | bytes 3149824 | tf_op jit(solution)/shard_map/dot_general | solution.py:34
  108.4 0.1 reshape.10
  108.5 0.6 reduce_sum.19
  (1 shorter events, 0.0 us)
Async XLA Ops:
  0.0 30.6 %copy-start = (bf16[512,1848]{0,1:T(8,128)(2,1)S(1)}, bf16[512,1848]{0,1:T(8,128)(2,1)}, u32[]{:S(2)}) copy-start(bf16[512,1848]{0,1:T(8,128)(2,1)} %param.9) | copy-start | bytes 5677060
  30.6 1.3 %copy-start.1 = (bf16[512,512]{1,0:T(8,128)(2,1)S(1)}, bf16[512,512]{1,0:T(8,128)(2,1)}, u32[]{:S(2)}) copy-start(bf16[512,512]{1,0:T(8,128)(2,1)} %param.8) | copy-start | bytes 1572868
  31.9 74.1 %copy-start.2 = (bf16[512,512]{1,0:T(8,128)(2,1)S(1)}, bf16[512,512]{1,0:T(8,128)(2,1)}, u32[]{:S(2)}) copy-start(bf16[512,512]{1,0:T(8,128)(2,1)} %param.15) | copy-start | bytes 1572868

commit v4 on v3

--- a/solution.py
+++ b/solution.py
@@ -20,10 +20,10 @@
     depth = basis_in.shape[0]
     own = jnp.concatenate([basis_in.T, basis_out.T], axis=1)
     own = (own.astype(f32) * LIFT).astype(f16)
-    basis = lax.all_gather(own, ("y", "x", "c"), axis=0, tiled=True).astype(bf16)
-    right = (rotate(out_grads, basis[:, depth:]) * (UP_OUT / LIFT)).astype(f16)
+    basis = lax.all_gather(own, ("y", "x", "c"), axis=0, tiled=True)
+    right = (rotate(out_grads, basis[:, depth:].astype(bf16)) * (UP_OUT / LIFT)).astype(f16)
     basis, right = lax.optimization_barrier((basis, right))
-    left = (rotate(activations, basis[:, :depth]) * (UP_IN / LIFT)).astype(f16)
+    left = (rotate(activations, basis[:, :depth].astype(bf16)) * (UP_IN / LIFT)).astype(f16)
     left, right = lax.psum((left, right), "z")
     position = lax.broadcasted_iota(jnp.int32, (right.shape[0], 1), 0)
     counted = (position < lengths[0]).astype(f32)

time: 109 us -> 109 us (level)
  no operation moved by 1% of the time
where the time goes in v4:
time: 109 us
  blocking collectives  102 us (94%)
  matrix products  4.18 us (4%)
  other arithmetic  1.62 us (1%)
    psum x1, blocking collectives, shards(): left, right = lax.psum((left, right), 'z')  72.9 us
    all_gather x1, blocking collectives, shards(): basis = lax.all_gather(own, ('y', 'x', 'c'), axis=0, tiled=True)  29.3 us
    dot_general x1, matrix products, shards(): weighted = jnp.dot(scaled, query_out, preferred_element_type=f32)  2.45 us

profile of v4, /device:TPU:2, one launch (start us, length us, event | category | flops | bytes accessed | tf_op | source)
XLA Modules:
  0.0 108.8 jit_solution(5327034675611320623)
XLA Ops:
  0.0 0.0 copy-start
  0.0 1.0 multiply_convert_fusion.6
  1.0 29.3 %all-gather.1 = f16[512,2360]{1,0:T(8,128)(2,1)S(1)} all-gather(f16[16,2360]{1,0:T(8,128)(2,1)S(1)} %multiply_convert_fusion.6), channel_id=1, replica_groups=mesh['y'=4,'x'=4,'c'=2,'z'=16] {'y','x','c'}, dimensions={0}, use_global_device_ids=true | all-gather | bytes 2492160 | tf_op jit(solution)/shard_map/all_gather | solution.py:23
  30.3 0.0 copy-done
  30.3 0.0 copy-start.1
  30.3 1.3 %fusion.6 = f16[512,512]{0,1:T(8,128)(2,1)S(1)} fusion(bf16[512,1848]{0,1:T(8,128)(2,1)S(1)} %copy-done, f16[512,2360]{1,0:T(8,128)(2,1)S(1)} %all-gather.1), kind=kOutput, calls=%fused_computation.10 | convolution fusion | flops 970354688 | bytes 4382720 | tf_op jit(solution)/shard_map/dot_general | solution.py:15
  31.6 0.0 copy-done.1
  31.6 0.0 copy-start.2
  31.6 0.5 fusion.2
  32.1 72.9 %all-reduce.2 = (u32[32768,4]{0,1:T(4,128)}, u32[32768,4]{0,1:T(4,128)}) all-reduce(u32[32768,4]{0,1:T(4,128)S(1)} %bitcast.18, u32[32768,4]{0,1:T(4,128)S(1)} %bitcast.17), channel_id=1, replica_groups=mesh['y'=4,'x'=4,'c'=2,'z'=16] {'z'}, use_global_device_ids=true, to_apply=%region_0.0.clone | all-reduce | flops 262144 | bytes 2097152 | tf_op jit(solution)/shard_map/psum | solution.py:27
  105.7 0.0 copy-done.2
  105.7 2.4 %fusion.5 = f32[512]{0:T(512)S(1)} fusion(bf16[512,512]{1,0:T(8,128)(2,1)S(1)} %copy-done.2, bf16[512,512]{1,0:T(8,128)(2,1)} %param.14, f32[512,512]{1,0:T(8,128)} %param.12, f16[512,512]{0,1:T(8,128)(2,1)} %bitcast.21, f16[512,512]{0,1:T(8,128)(2,1)} %bitcast.22, f32[512]{0:T(512)S(1)} %fusion.14), kind=kOutput, calls=%fused_computation.9 | convolution fusion | flops 540016128 | bytes 3149824 | tf_op jit(solution)/shard_map/dot_general | solution.py:34
  108.1 0.1 reshape.10
  108.2 0.6 reduce_sum.19
  (1 shorter events, 0.0 us)
Async XLA Ops:
  0.0 30.3 %copy-start = (bf16[512,1848]{0,1:T(8,128)(2,1)S(1)}, bf16[512,1848]{0,1:T(8,128)(2,1)}, u32[]{:S(2)}) copy-start(bf16[512,1848]{0,1:T(8,128)(2,1)} %param.9) | copy-start | bytes 5677060
  30.3 1.3 %copy-start.1 = (bf16[512,512]{1,0:T(8,128)(2,1)S(1)}, bf16[512,512]{1,0:T(8,128)(2,1)}, u32[]{:S(2)}) copy-start(bf16[512,512]{1,0:T(8,128)(2,1)} %param.8) | copy-start | bytes 1572868
  31.6 74.1 %copy-start.2 = (bf16[512,512]{1,0:T(8,128)(2,1)S(1)}, bf16[512,512]{1,0:T(8,128)(2,1)}, u32[]{:S(2)}) copy-start(bf16[512,512]{1,0:T(8,128)(2,1)} %param.15) | copy-start | bytes 1572868
